TPU v7x, 32 devices: a whole 2x2x4 slice. The times are simulated.
32 devices in a mesh: row: 8 (over y, x, core), col: 4 (over z).
Axes of the slice: x: 2, y: 2, z: 4, core: 2. Of those that a mesh axis runs over, the one named last changes fastest.
Arguments:
- activations: bfloat16 [256, 64, 5120], P(('row', 'col')), may hold values from -6 to 6
- out_grads: bfloat16 [256, 64, 8192], P(('row', 'col')), may hold values from -6 to 6
- lengths: int32 [256], P(('row', 'col')), may hold values from 16 to 64
- proj_in: bfloat16 [5120, 128], replicated, may hold values from -0.078125 to 0.078125
- proj_out: bfloat16 [8192, 128], replicated, may hold values from -0.0625 to 0.0625
Outputs:
- fisher: float32 [16384, 16384], P('row', 'col')
All inputs are finite; a program needn't handle non-finite values.
Results may differ from a plain program's by a relative error of at most 0.0068.
Values may be sent and summed in bfloat16 or wider, within the bound.
A program may use at most 128 MiB of HBM per device.

v0:
```python
import jax
import jax.numpy as jnp
from jax import lax
from jax.sharding import PartitionSpec as P

L = 64


def contract(left, right):
    return lax.dot_general(
        left, right, (((0,), (0,)), ((), ())), preferred_element_type=jnp.float32
    )


def on_device(activations, out_grads, lengths, proj_in, proj_out):
    local_ex = activations.shape[0]
    width = proj_in.shape[1]
    order = width * width
    in_factors = jnp.dot(
        activations.reshape(local_ex * L, -1), proj_in, preferred_element_type=jnp.float32
    ).astype(jnp.bfloat16)
    out_raw = jnp.dot(
        out_grads.reshape(local_ex * L, -1), proj_out, preferred_element_type=jnp.float32
    )
    positions = lax.broadcasted_iota(jnp.int32, (local_ex, L), 1)
    valid = (positions < lengths[:, None]).astype(jnp.float32).reshape(local_ex * L, 1)
    out_factors = (out_raw * valid).astype(jnp.bfloat16)
    grads = jnp.einsum(
        "eti,etj->eij",
        out_factors.reshape(local_ex, L, width),
        in_factors.reshape(local_ex, L, width),
        preferred_element_type=jnp.float32,
    )
    grads = (grads * (1.0 / jnp.sqrt(jnp.float32(L)))).astype(jnp.bfloat16).reshape(local_ex, order)
    n_row = lax.axis_size("row")
    n_col = lax.axis_size("col")
    row_width = order // n_row
    total_ex = local_ex * n_row * n_col
    row_part = lax.all_to_all(grads, "row", split_axis=1, concat_axis=0, tiled=True)
    row_all = lax.all_gather(row_part, "col", axis=0, tiled=True)
    row_all = (
        row_all.reshape(n_col, n_row, local_ex, row_width)
        .transpose(1, 0, 2, 3)
        .reshape(total_ex, row_width)
    )
    col_part = lax.all_to_all(grads, "col", split_axis=1, concat_axis=0, tiled=True)
    fisher = contract(row_all, lax.all_gather(col_part, "row", axis=0, tiled=True))
    return fisher * (1.0 / jnp.sqrt(jnp.float32(total_ex)))


def solution(mesh):
    placed = (
        P(("row", "col"), None, None),
        P(("row", "col"), None, None),
        P(("row", "col")),
        P(),
        P(),
    )
    return jax.shard_map(
        on_device, mesh=mesh, in_specs=placed, out_specs=P("row", "col"), check_vma=False
    )
```

profile of v0, /device:TPU:0, one launch (start us, length us, event | category | flops | bytes accessed | tf_op | source)
XLA Modules:
  0.0 110.9 jit_solution(7016804139801036429)
XLA Ops:
  6.5 0.0 copy-start
  6.5 0.0 all-gather.3.cloned.1.call-start
  6.5 0.9 fusion.2
  7.4 0.1 reshape.52
  7.5 4.4 %convolution_convert_fusion = bf16[512,128]{1,0:T(8,128)(2,1)S(1)} fusion(bf16[512,5120]{1,0:T(8,128)(2,1)} %bitcast.29, bf16[5120,128]{1,0:T(8,128)(2,1)} %param.8), kind=kOutput, calls=%fused_computation.5 | convolution fusion | flops 671154176 | bytes 6684672 | tf_op jit(solution)/shard_map/dot_general | solution.py:19
  11.9 0.0 copy-done
  11.9 5.7 %fusion.1 = bf16[512,128]{1,0:T(8,128)(2,1)S(1)} fusion(bf16[512,8192]{1,0:T(8,128)(2,1)} %bitcast.28, bf16[8192,128]{1,0:T(8,128)(2,1)S(1)} %copy-done, f32[512]{0:T(512)S(1)} %reshape.52), kind=kOutput, calls=%fused_computation.4 | convolution fusion | flops 1073872896 | bytes 10618880 | tf_op jit(solution)/shard_map/dot_general | solution.py:22
  17.6 0.3 fusion
  17.9 0.1 all_to_all.28
  18.0 0.2 copy.6
  18.2 12.0 %all_to_all.38 = bf16[8,8,2048]{2,0,1:T(8,128)(2,1)} all-to-all(bf16[8,8,2048]{2,0,1:T(8,128)(2,1)S(1)} %copy.6), channel_id=1, replica_groups=mesh['row'=8,'col'=4] {'row'}, dimensions={1} | all-to-all | bytes 524288 | tf_op jit(solution)/shard_map/all_to_all | solution.py:39
  30.2 0.0 all-gather.3.cloned.1.call-update
  30.2 0.0 all-gather.5.cloned.1.call-start
  30.3 0.1 all_to_all.32
  30.3 0.2 copy.8
  30.5 18.1 %all_to_all.39 = bf16[8,4,4096]{2,0,1:T(8,128)(2,1)} all-to-all(bf16[8,4,4096]{2,0,1:T(8,128)(2,1)S(1)} %copy.8), channel_id=1, replica_groups=mesh['row'=8,'col'=4] {'col'}, dimensions={1} | all-to-all | bytes 524288 | tf_op jit(solution)/shard_map/all_to_all | solution.py:46
  48.6 0.0 all-gather.5.cloned.1.call-update
  48.6 12.0 %all-gather.3.cloned.1.call-done = bf16[256,2048]{1,0:T(8,128)(2,1)} async-done(((bf16[64,2048]{1,0:T(8,128)(2,1)}), bf16[256,2048]{1,0:T(8,128)(2,1)}) %all-gather.3.cloned.1.call-update) | async-done | bytes 1048592 | tf_op jit(solution)/shard_map/all_gather | solution.py:40
  60.6 1.3 %copy.7 = bf16[4,8,8,2048]{3,2,0,1:T(8,128)(2,1)S(1)} copy(bf16[4,8,8,2048]{3,2,1,0:T(8,128)(2,1)} %bitcast.23) | data formatting | bytes 2097152 | tf_op jit(solution)/shard_map/reshape | solution.py:42
  61.9 26.5 %all-gather.5.cloned.1.call-done = bf16[256,4096]{1,0:T(8,128)(2,1)} async-done(((bf16[32,4096]{1,0:T(8,128)(2,1)}), bf16[256,4096]{1,0:T(8,128)(2,1)}) %all-gather.5.cloned.1.call-update) | async-done | bytes 2097168 | tf_op jit(solution)/shard_map/all_gather | solution.py:47
  88.4 15.7 %broadcast_multiply_fusion = f32[2048,4096]{1,0:T(8,128)} fusion(bf16[256,2048]{1,0:T(8,128)(2,1)S(1)} %bitcast.22, bf16[256,4096]{1,0:T(8,128)(2,1)} %all-gather.5.cloned.1.call-done), kind=kOutput, calls=%fused_computation | convolution fusion | flops 4303355904 | bytes 36700160 | tf_op jit(solution)/shard_map/dot_general | solution.py:10
Async XLA Ops:
  6.5 5.3 %copy-start = (bf16[8192,128]{1,0:T(8,128)(2,1)S(1)}, bf16[8192,128]{1,0:T(8,128)(2,1)}, u32[]{:S(2)}) copy-start(bf16[8192,128]{1,0:T(8,128)(2,1)} %param.9) | copy-start | bytes 6291460
  6.5 54.1 %all-gather.3.cloned.1.call-start = ((), (), s32[]{:S(2)}) async-start(), calls=%async_computation.2 | async-start | bytes 1310720 | tf_op jit(solution)/shard_map/all_gather | solution.py:40
  30.2 58.2 %all-gather.5.cloned.1.call-start = ((), (), s32[]{:S(2)}) async-start(), calls=%async_computation.3 | async-start | bytes 2359296 | tf_op jit(solution)/shard_map/all_gather | solution.py:47
Sparse Core Ops, SparseCore 0:
  30.3 30.2 all-gather.2
  62.5 25.8 all-gather.4
where the time goes:
time: 111 us
  waiting for transfers between devices  38.5 us (35%)
  blocking collectives  30.1 us (27%)
  matrix products  26 us (23%)
  between operations  13.5 us (12%)
  local copies, waits for them, and re-layouts  1.86 us (2%)
    all_gather x1, waiting for transfers between devices, on_device(): lax.all_gather(col_part, 'row', axis=0, tiled=True)  26.5 us
    all_to_all x1, blocking collectives, on_device(): lax.all_to_all(grads, 'col', split_axis=1, concat_axis=0, tiled=True)  18.1 us
    dot_general x1, matrix products, contract(): lax.dot_general(left, right, (((0,), (0,)), ((), ())), preferred_element_...  15.7 us
    all_to_all x1, blocking collectives, on_device(): lax.all_to_all(grads, 'row', split_axis=1, concat_axis=0, tiled=True)  12 us
    all_gather x1, waiting for transfers between devices, on_device(): row_all = lax.all_gather(row_part, 'col', axis=0, tiled=True)  12 us
    dot_general x1, matrix products, on_device(): jnp.dot(out_grads.reshape(local_ex * L, -1), proj_out, preferred_element_...  5.71 us
    dot_general x1, matrix products, on_device(): jnp.dot(activations.reshape(local_ex * L, -1), proj_in, preferred_element...  4.38 us
  transfers between devices with their start and end apart: 2, of which 2 were waited for; matrix products, arithmetic and copies ran while one was open for 1% of the time, Pallas kernels for 0%

commit v1 on v0

v1 whole, which is shorter than its diff:
```python
import functools

import jax
import jax.numpy as jnp
from jax import lax
from jax.experimental import pallas as pl
from jax.experimental.pallas import tpu as pltpu
from jax.sharding import PartitionSpec as P

L = 64
CORES = 2
MESH = pl.DeviceIdType.MESH
MIB = 1024 * 1024


def project_kernel(steps, lengths, act, og, w_in, w_out, in_f, out_f, in_acc, out_acc):
    step = pl.program_id(0)
    in_part = jnp.dot(act[...], w_in[...], preferred_element_type=jnp.float32)
    out_part = jnp.dot(og[...], w_out[...], preferred_element_type=jnp.float32)

    @pl.when(step == 0)
    def _():
        in_acc[...] = in_part
        out_acc[...] = out_part

    @pl.when(step > 0)
    def _():
        in_acc[...] += in_part
        out_acc[...] += out_part

    @pl.when(step == steps - 1)
    def _():
        in_f[...] = in_acc[...].astype(in_f.dtype)
        place = lax.broadcasted_iota(jnp.int32, (L, out_f.shape[1]), 0)
        for e in range(out_f.shape[0] // L):
            rows = pl.ds(e * L, L)
            kept = jnp.where(place < lengths[e], out_acc[rows, :], 0.0)
            out_f[rows, :] = kept.astype(out_f.dtype)


def project(activations, out_grads, lengths, proj_in, proj_out):
    steps = 4
    tokens, width = activations.shape[0], proj_in.shape[1]
    deep_in, deep_out = activations.shape[1] // steps, out_grads.shape[1] // steps
    factors = jax.ShapeDtypeStruct((tokens, width), jnp.bfloat16)
    whole = pl.BlockSpec((tokens, width), lambda s: (0, 0))
    return pl.pallas_call(
        functools.partial(project_kernel, steps),
        grid=(steps,),
        in_specs=[
            pl.BlockSpec(memory_space=pltpu.SMEM),
            pl.BlockSpec((tokens, deep_in), lambda s: (0, s)),
            pl.BlockSpec((tokens, deep_out), lambda s: (0, s)),
            pl.BlockSpec((deep_in, width), lambda s: (s, 0)),
            pl.BlockSpec((deep_out, width), lambda s: (s, 0)),
        ],
        out_specs=[whole, whole],
        out_shape=[factors, factors],
        scratch_shapes=[pltpu.VMEM((tokens, width), jnp.float32)] * 2,
        compiler_params=pltpu.CompilerParams(vmem_limit_bytes=32 * MIB),
    )(lengths, activations, out_grads, proj_in, proj_out)


def exchange_kernel(
    n, in_f, out_f, row_ref, col_ref,
    in_peer, out_peer, wide, blocks,
    peer_s, peer_r, c1_s, c1_r, r1_s, r1_r, r2_s, r2_r, c2_s, c2_r, fw_s, fw_r, own_s,
):
    r, c = lax.axis_index("row"), lax.axis_index("col")
    k, m = r // CORES, r % CORES
    peer = (k * CORES + 1 - m, c)
    width = in_f.shape[1]
    local_ex = in_f.shape[0] // L
    pair_ex = CORES * local_ex
    per_block = blocks.shape[2] // width

    def turn(start, d):
        return lax.rem(start + d + n, n)

    def send(src, dst, s, t, who):
        copy = pltpu.make_async_remote_copy(
            src_ref=src, dst_ref=dst, send_sem=s, recv_sem=t, device_id=who, device_id_type=MESH
        )
        copy.start()
        return copy

    barrier = pltpu.get_barrier_semaphore()
    pl.semaphore_signal(barrier, inc=1, device_id=peer, device_id_type=MESH)
    for d in range(1, n):
        pl.semaphore_signal(barrier, inc=1, device_id=(turn(k, d) * CORES + m, c), device_id_type=MESH)
        pl.semaphore_signal(barrier, inc=1, device_id=(r, turn(c, d)), device_id_type=MESH)
    pl.semaphore_wait(barrier, 2 * n - 1)

    swaps = [
        send(in_f, in_peer, peer_s.at[0], peer_r.at[0], peer),
        send(out_f, out_peer, peer_s.at[1], peer_r.at[1], peer),
    ]

    def outer(ins, outs, core):
        for e in range(local_ex):
            rows = pl.ds(e * L, L)
            grad = lax.dot_general(
                outs[rows, :], ins[rows, :], (((0,), (0,)), ((), ())), preferred_element_type=jnp.float32
            )
            place = pl.multiple_of((core * local_ex + e) * width, width)
            wide[pl.ds(place, width), :] = grad * (1.0 / jnp.sqrt(jnp.float32(L)))

    outer(in_f, out_f, m)
    for copy in swaps:
        copy.wait()
    outer(in_peer, out_peer, 1 - m)

    for q in range(n):
        for i in range(per_block):
            first = (q * CORES + m) * per_block + i
            blocks[q, :, i * width : (i + 1) * width] = wide[
                pl.ds(first, pair_ex, stride=width), :
            ].astype(blocks.dtype)

    to_col, to_row = [], []
    for d in range(1, n):
        q = turn(c, d)
        to_col.append(send(blocks.at[q], col_ref.at[m, c, k], c1_s.at[d], c1_r.at[d], (r, q)))
        q = turn(k, d)
        to_row.append(send(blocks.at[q], row_ref.at[c, k], r1_s.at[d], r1_r.at[d], (q * CORES + m, c)))
    own = [
        pltpu.make_async_copy(blocks.at[k], row_ref.at[c, k], own_s.at[0]),
        pltpu.make_async_copy(blocks.at[c], col_ref.at[m, c, k], own_s.at[1]),
    ]
    for copy in own:
        copy.start()

    for copy in to_row:
        copy.wait()
    own[0].wait()
    along = [
        send(row_ref.at[c], row_ref.at[c], r2_s.at[d], r2_r.at[d], (r, turn(c, d)))
        for d in range(1, n)
    ]

    for copy in to_col:
        copy.wait()
    own[1].wait()
    mine = col_ref.at[m, :, k]
    across = [
        send(mine, mine, c2_s.at[d], c2_r.at[d], (turn(k, d) * CORES + m, c)) for d in range(1, n)
    ]
    passed = [send(mine, mine, fw_s.at[0], fw_r.at[0], peer)]
    for d in range(1, n):
        across[d - 1].wait_recv()
        piece = col_ref.at[m, :, turn(k, -d)]
        passed.append(send(piece, piece, fw_s.at[d], fw_r.at[d], peer))
    for copy in across:
        copy.wait_send()
    for copy in along:
        copy.wait()
    for copy in passed:
        copy.wait()


def exchange(in_f, out_f, n_row, n_col):
    n = n_col
    assert n_row == CORES * n
    tokens, width = in_f.shape
    pair_ex = CORES * (tokens // L)
    block = width * width // n_row
    dma = pltpu.SemaphoreType.DMA
    anywhere = pl.BlockSpec(memory_space=pl.ANY)
    return pl.pallas_call(
        functools.partial(exchange_kernel, n),
        in_specs=[pl.BlockSpec(memory_space=pltpu.VMEM)] * 2,
        out_specs=[anywhere, anywhere],
        out_shape=[
            jax.ShapeDtypeStruct((n, n, pair_ex, block), jnp.bfloat16),
            jax.ShapeDtypeStruct((CORES, n, n, pair_ex, block), jnp.bfloat16),
        ],
        scratch_shapes=[
            pltpu.VMEM((tokens, width), jnp.bfloat16),
            pltpu.VMEM((tokens, width), jnp.bfloat16),
            pltpu.VMEM((pair_ex * width, width), jnp.float32),
            pltpu.VMEM((n, pair_ex, block), jnp.bfloat16),
            dma((2,)), dma((2,)),
        ]
        + [dma((n,))] * 10
        + [dma((2,))],
        compiler_params=pltpu.CompilerParams(
            collective_id=0, has_side_effects=True, vmem_limit_bytes=32 * MIB
        ),
    )(in_f, out_f)


def fisher_kernel(scale, left, right, out):
    out[...] = scale * lax.dot_general(
        left[...], right[0], (((0,), (0,)), ((), ())), preferred_element_type=jnp.float32
    )


def fisher(row_all, col_all):
    total, rows = row_all.shape
    halves, _, block = col_all.shape
    tile = min(256, rows)
    return pl.pallas_call(
        functools.partial(fisher_kernel, 1.0 / total**0.5),
        grid=(halves, rows // tile),
        in_specs=[
            pl.BlockSpec((total, tile), lambda h, i: (0, i)),
            pl.BlockSpec((1, total, block), lambda h, i: (h, 0, 0)),
        ],
        out_specs=pl.BlockSpec((tile, block), lambda h, i: (i, h)),
        out_shape=jax.ShapeDtypeStruct((rows, halves * block), jnp.float32),
        compiler_params=pltpu.CompilerParams(vmem_limit_bytes=32 * MIB),
    )(row_all, col_all)


def on_device(activations, out_grads, lengths, proj_in, proj_out):
    tokens = activations.shape[0] * L
    n_row = lax.axis_size("row")
    n_col = lax.axis_size("col")
    in_f, out_f = project(
        activations.reshape(tokens, -1), out_grads.reshape(tokens, -1), lengths, proj_in, proj_out
    )
    row_all, col_all = exchange(in_f, out_f, n_row, n_col)
    block = row_all.shape[-1]
    return fisher(row_all.reshape(-1, block), col_all.reshape(CORES, -1, block))


def solution(mesh):
    placed = (
        P(("row", "col"), None, None),
        P(("row", "col"), None, None),
        P(("row", "col")),
        P(),
        P(),
    )
    return jax.shard_map(
        on_device, mesh=mesh, in_specs=placed, out_specs=P("row", "col"), check_vma=False
    )
```

time: 111 us -> 66.2 us (0.60)
  the two profiles are of different devices: /device:TPU:0 before, /device:TPU:8 now
where the time goes in v1:
time: 66.2 us; the launch traced here: 66 us
  Pallas kernels  56.5 us (85%)
  local copies, waits for them, and re-layouts  9.43 us (14%)
    pallas_call x1, Pallas kernels, exchange(): pl.pallas_call(functools.partial(exchange_kernel, n), in_specs=[pl.BlockS...  35.7 us
    pallas_call x1, Pallas kernels, fisher(): pl.pallas_call(functools.partial(fisher_kernel, 1.0 / total ** 0.5), grid...  15.1 us
    unnamed x10, local copies, waits for them, and re-layouts  9.43 us
    pallas_call x1, Pallas kernels, project(): pl.pallas_call(functools.partial(project_kernel, steps), grid=(steps,), i...  5.75 us

profile of v1, /device:TPU:8, one launch (start us, length us, event | category | flops | bytes accessed | tf_op | source)
XLA Modules:
  0.0 66.0 jit_solution(193249187770297448)
XLA Ops:
  0.0 0.0 copy-start
  0.0 3.4 %copy-done = bf16[8,64,8192]{2,1,0:T(8,128)(2,1)S(1)} copy-done((bf16[8,64,8192]{2,1,0:T(8,128)(2,1)S(1)}, bf16[8,64,8192]{2,1,0:T(8,128)(2,1)}, u32[]{:S(2)}) %copy-start) | copy-done | bytes 8388632
  3.4 0.0 copy-start.1
  3.4 2.5 %copy-done.1 = bf16[8,64,5120]{2,1,0:T(8,128)(2,1)S(1)} copy-done((bf16[8,64,5120]{2,1,0:T(8,128)(2,1)S(1)}, bf16[8,64,5120]{2,1,0:T(8,128)(2,1)}, u32[]{:S(2)}) %copy-start.1) | copy-done | bytes 5242904
  5.9 0.0 copy-start.2
  5.9 1.6 %copy-done.2 = bf16[8192,128]{1,0:T(8,128)(2,1)S(1)} copy-done((bf16[8192,128]{1,0:T(8,128)(2,1)S(1)}, bf16[8192,128]{1,0:T(8,128)(2,1)}, u32[]{:S(2)}) %copy-start.2) | copy-done | bytes 2097176
  7.5 0.0 copy-start.3
  7.5 1.3 %copy-done.3 = bf16[5120,128]{1,0:T(8,128)(2,1)S(1)} copy-done((bf16[5120,128]{1,0:T(8,128)(2,1)S(1)}, bf16[5120,128]{1,0:T(8,128)(2,1)}, u32[]{:S(2)}) %copy-start.3) | copy-done | bytes 1310744
  8.8 0.0 copy-start.4
  8.8 0.7 copy-done.4
  9.4 5.7 %shard_map.55 = (bf16[512,128]{1,0:T(8,128)(2,1)S(1)}, bf16[512,128]{1,0:T(8,128)(2,1)S(1)}) custom-call(s32[8]{0:T(128)S(1)} %copy-done.4, bf16[512,5120]{1,0:T(8,128)(2,1)S(1)} %bitcast.5, bf16[512,8192]{1,0:T(8,128)(2,1)S(1)} %bitcast.4, bf16[5120,128]{1,0:T(8,128)(2,1)S(1)} %copy-done.3, bf16[8192,128]{1,0:T(8,128)(2,1)S(1)} %copy-done.2), custom_call_target="tpu_custom_call" | custom-call | tf_op jit(solution)/shard_map/pallas_call | solution.py:47
  15.2 35.7 %shard_map.56 = (bf16[4,4,16,2048]{3,2,1,0:T(8,128)(2,1)S(1)}, bf16[2,4,4,16,2048]{4,3,2,1,0:T(8,128)(2,1)S(1)}) custom-call(bf16[512,128]{1,0:T(8,128)(2,1)S(1)} %get-tuple-element.9.in_f, bf16[512,128]{1,0:T(8,128)(2,1)S(1)} %get-tuple-element.10.out_f), custom_call_target="tpu_custom_call" | custom-call | tf_op jit(solution)/shard_map/pallas_call | solution.py:169
  50.9 15.1 %shard_map.57 = f32[2048,4096]{1,0:T(8,128)} custom-call(bf16[256,2048]{1,0:T(8,128)(2,1)S(1)} %bitcast.7, bf16[2,256,2048]{2,1,0:T(8,128)(2,1)S(1)} %bitcast.6), custom_call_target="tpu_custom_call" | custom-call | tf_op jit(solution)/shard_map/pallas_call | solution.py:202
Async XLA Ops:
  0.0 3.4 %copy-start = (bf16[8,64,8192]{2,1,0:T(8,128)(2,1)S(1)}, bf16[8,64,8192]{2,1,0:T(8,128)(2,1)}, u32[]{:S(2)}) copy-start(bf16[8,64,8192]{2,1,0:T(8,128)(2,1)} %param.6) | copy-start | bytes 25165828
  3.4 2.5 %copy-start.1 = (bf16[8,64,5120]{2,1,0:T(8,128)(2,1)S(1)}, bf16[8,64,5120]{2,1,0:T(8,128)(2,1)}, u32[]{:S(2)}) copy-start(bf16[8,64,5120]{2,1,0:T(8,128)(2,1)} %param.5) | copy-start | bytes 15728644
  5.9 1.6 %copy-start.2 = (bf16[8192,128]{1,0:T(8,128)(2,1)S(1)}, bf16[8192,128]{1,0:T(8,128)(2,1)}, u32[]{:S(2)}) copy-start(bf16[8192,128]{1,0:T(8,128)(2,1)} %w_out.1) | copy-start | bytes 6291460
  7.5 1.3 %copy-start.3 = (bf16[5120,128]{1,0:T(8,128)(2,1)S(1)}, bf16[5120,128]{1,0:T(8,128)(2,1)}, u32[]{:S(2)}) copy-start(bf16[5120,128]{1,0:T(8,128)(2,1)} %w_in.1) | copy-start | bytes 3932164
  8.8 0.7 copy-start.4

commit v2 on v1

--- a/solution.py
+++ b/solution.py
@@ -57,14 +57,14 @@
         out_specs=[whole, whole],
         out_shape=[factors, factors],
         scratch_shapes=[pltpu.VMEM((tokens, width), jnp.float32)] * 2,
-        compiler_params=pltpu.CompilerParams(vmem_limit_bytes=32 * MIB),
+        compiler_params=pltpu.CompilerParams(vmem_limit_bytes=60 * MIB),
     )(lengths, activations, out_grads, proj_in, proj_out)
 
 
 def exchange_kernel(
     n, in_f, out_f, row_ref, col_ref,
     in_peer, out_peer, wide, blocks,
-    peer_s, peer_r, c1_s, c1_r, r1_s, r1_r, r2_s, r2_r, c2_s, c2_r, fw_s, fw_r, own_s,
+    peer_s, peer_r, c1_s, c1_r, r1_s, r1_r, line_s, line_r, c2_s, c2_r, fw_s, fw_r, own_s,
 ):
     r, c = lax.axis_index("row"), lax.axis_index("col")
     k, m = r // CORES, r % CORES
@@ -130,13 +130,57 @@
     for copy in own:
         copy.start()
 
+    half = n // 2
+
+    def hop(way, t, p):
+        shard = row_ref.at[c - way * t, pl.ds(p * half, half)]
+        w = (way + 1) // 2
+        return pltpu.make_async_remote_copy(
+            src_ref=shard,
+            dst_ref=shard,
+            send_sem=line_s.at[w, t, p],
+            recv_sem=line_r.at[w, t, p],
+            device_id=(r, c + way),
+            device_id_type=MESH,
+        )
+
+    def arrival(way, t, p):
+        shard = row_ref.at[c - way * t, pl.ds(p * half, half)]
+        w = (way + 1) // 2
+        return pltpu.make_async_remote_copy(
+            src_ref=shard,
+            dst_ref=shard,
+            send_sem=line_s.at[w, t - 1, p],
+            recv_sem=line_r.at[w, t - 1, p],
+            device_id=(r, c - way),
+            device_id_type=MESH,
+        )
+
+    def comes(way, t):
+        return c - t >= 0 if way > 0 else c + t <= n - 1
+
+    def goes(way):
+        return c <= n - 2 if way > 0 else c >= 1
+
+    def relay(t):
+        for p in range(2):
+            for way in (1, -1):
+                if t > 0:
+
+                    @pl.when(comes(way, t))
+                    def _(way=way, p=p):
+                        arrival(way, t, p).wait_recv()
+
+                if t < n - 1:
+
+                    @pl.when(jnp.logical_and(comes(way, t), goes(way)))
+                    def _(way=way, p=p):
+                        hop(way, t, p).start()
+
     for copy in to_row:
         copy.wait()
     own[0].wait()
-    along = [
-        send(row_ref.at[c], row_ref.at[c], r2_s.at[d], r2_r.at[d], (r, turn(c, d)))
-        for d in range(1, n)
-    ]
+    relay(0)
 
     for copy in to_col:
         copy.wait()
@@ -147,13 +191,20 @@
     ]
     passed = [send(mine, mine, fw_s.at[0], fw_r.at[0], peer)]
     for d in range(1, n):
+        relay(d)
         across[d - 1].wait_recv()
         piece = col_ref.at[m, :, turn(k, -d)]
         passed.append(send(piece, piece, fw_s.at[d], fw_r.at[d], peer))
     for copy in across:
         copy.wait_send()
-    for copy in along:
-        copy.wait()
+    for t in range(n - 1):
+        for way in (1, -1):
+
+            @pl.when(jnp.logical_and(comes(way, t), goes(way)))
+            def _(way=way, t=t):
+                for p in range(2):
+                    hop(way, t, p).wait_send()
+
     for copy in passed:
         copy.wait()
 
@@ -181,7 +232,9 @@
             pltpu.VMEM((n, pair_ex, block), jnp.bfloat16),
             dma((2,)), dma((2,)),
         ]
-        + [dma((n,))] * 10
+        + [dma((n,))] * 4
+        + [dma((2, n - 1, 2))] * 2
+        + [dma((n,))] * 4
         + [dma((2,))],
         compiler_params=pltpu.CompilerParams(
             collective_id=0, has_side_effects=True, vmem_limit_bytes=32 * MIB
@@ -189,26 +242,63 @@
     )(in_f, out_f)
 
 
-def fisher_kernel(scale, left, right, out):
-    out[...] = scale * lax.dot_general(
+def fisher_kernel(scale, slots, parts, left, right, out, held, sems):
+    h, i = pl.program_id(0), pl.program_id(1)
+    tiles = pl.num_programs(1)
+    steps = pl.num_programs(0) * tiles
+    step = h * tiles + i
+    _, tile, block = held.shape
+    piece = tile // parts
+
+    def writes(s):
+        slot = lax.rem(s, slots)
+        top, side = lax.rem(s, tiles) * tile, lax.div(s, tiles) * block
+        return [
+            pltpu.make_async_copy(
+                held.at[slot, pl.ds(p * piece, piece)],
+                out.at[pl.ds(top + p * piece, piece), pl.ds(pl.multiple_of(side, block), block)],
+                sems.at[slot, p],
+            )
+            for p in range(parts)
+        ]
+
+    @pl.when(step >= slots)
+    def _():
+        for copy in writes(step - slots):
+            copy.wait()
+
+    slot = lax.rem(step, slots)
+    held[slot] = scale * lax.dot_general(
         left[...], right[0], (((0,), (0,)), ((), ())), preferred_element_type=jnp.float32
     )
+    for copy in writes(step):
+        copy.start()
+
+    @pl.when(step == steps - 1)
+    def _():
+        for back in range(slots - 1, -1, -1):
+            for copy in writes(step - back):
+                copy.wait()
 
 
 def fisher(row_all, col_all):
     total, rows = row_all.shape
     halves, _, block = col_all.shape
-    tile = min(256, rows)
+    tile, slots, parts = min(256, rows // 4), 4, 2
     return pl.pallas_call(
-        functools.partial(fisher_kernel, 1.0 / total**0.5),
+        functools.partial(fisher_kernel, 1.0 / total**0.5, slots, parts),
         grid=(halves, rows // tile),
         in_specs=[
             pl.BlockSpec((total, tile), lambda h, i: (0, i)),
             pl.BlockSpec((1, total, block), lambda h, i: (h, 0, 0)),
         ],
-        out_specs=pl.BlockSpec((tile, block), lambda h, i: (i, h)),
+        out_specs=pl.BlockSpec(memory_space=pl.ANY),
         out_shape=jax.ShapeDtypeStruct((rows, halves * block), jnp.float32),
-        compiler_params=pltpu.CompilerParams(vmem_limit_bytes=32 * MIB),
+        scratch_shapes=[
+            pltpu.VMEM((slots, tile, block), jnp.float32),
+            pltpu.SemaphoreType.DMA((slots, parts)),
+        ],
+        compiler_params=pltpu.CompilerParams(vmem_limit_bytes=24 * MIB),
     )(row_all, col_all)
 
 

time: 66.2 us -> 54.6 us (0.82)
  the two profiles are of different devices: /device:TPU:8 before, /device:TPU:0 now
where the time goes in v2:
time: 54.6 us; the launch traced here: 54.5 us
  Pallas kernels  52.7 us (97%)
  local copies, waits for them, and re-layouts  1.81 us (3%)
    pallas_call x1, Pallas kernels, exchange(): pl.pallas_call(functools.partial(exchange_kernel, n), in_specs=[pl.BlockS...  32.5 us
    pallas_call x1, Pallas kernels, fisher(): pl.pallas_call(functools.partial(fisher_kernel, 1.0 / total ** 0.5, slots...  11.5 us
    pallas_call x1, Pallas kernels, project(): pl.pallas_call(functools.partial(project_kernel, steps), grid=(steps,), i...  8.75 us
    unnamed x4, local copies, waits for them, and re-layouts  1.81 us

profile of v2, /device:TPU:0, one launch (start us, length us, event | category | flops | bytes accessed | tf_op | source)
XLA Modules:
  0.0 54.5 jit_solution(4995694437105633901)
XLA Ops:
  0.0 8.7 %shard_map.55 = (bf16[512,128]{1,0:T(8,128)(2,1)}, bf16[512,128]{1,0:T(8,128)(2,1)}) custom-call(s32[8]{0:T(128)} %lengths.1, bf16[512,5120]{1,0:T(8,128)(2,1)} %bitcast.7, bf16[512,8192]{1,0:T(8,128)(2,1)} %bitcast.6, bf16[5120,128]{1,0:T(8,128)(2,1)} %w_in.1, bf16[8192,128]{1,0:T(8,128)(2,1)} %w_out.1), custom_call_target="tpu_custom_call" | custom-call | tf_op jit(solution)/shard_map/pallas_call | solution.py:47
  8.7 0.0 copy-start
  8.8 0.9 %copy-done = bf16[512,128]{1,0:T(8,128)(2,1)S(1)} copy-done((bf16[512,128]{1,0:T(8,128)(2,1)S(1)}, bf16[512,128]{1,0:T(8,128)(2,1)}, u32[]{:S(2)}) %copy-start) | copy-done | bytes 131096
  9.7 0.0 copy-start.1
  9.7 0.9 %copy-done.1 = bf16[512,128]{1,0:T(8,128)(2,1)S(1)} copy-done((bf16[512,128]{1,0:T(8,128)(2,1)S(1)}, bf16[512,128]{1,0:T(8,128)(2,1)}, u32[]{:S(2)}) %copy-start.1) | copy-done | bytes 131096
  10.6 32.5 %shard_map.56 = (bf16[4,4,16,2048]{3,2,1,0:T(8,128)(2,1)S(1)}, bf16[2,4,4,16,2048]{4,3,2,1,0:T(8,128)(2,1)S(1)}) custom-call(bf16[512,128]{1,0:T(8,128)(2,1)S(1)} %copy-done, bf16[512,128]{1,0:T(8,128)(2,1)S(1)} %copy-done.1), custom_call_target="tpu_custom_call" | custom-call | tf_op jit(solution)/shard_map/pallas_call | solution.py:220
  43.0 11.5 %shard_map.57 = f32[2048,4096]{1,0:T(8,128)} custom-call(bf16[256,2048]{1,0:T(8,128)(2,1)S(1)} %bitcast.5, bf16[2,256,2048]{2,1,0:T(8,128)(2,1)S(1)} %bitcast.4), custom_call_target="tpu_custom_call" | custom-call | tf_op jit(solution)/shard_map/pallas_call | solution.py:288
Async XLA Ops:
  8.7 0.9 %copy-start = (bf16[512,128]{1,0:T(8,128)(2,1)S(1)}, bf16[512,128]{1,0:T(8,128)(2,1)}, u32[]{:S(2)}) copy-start(bf16[512,128]{1,0:T(8,128)(2,1)} %get-tuple-element.9.in_f) | copy-start | bytes 393220
  9.7 0.9 %copy-start.1 = (bf16[512,128]{1,0:T(8,128)(2,1)S(1)}, bf16[512,128]{1,0:T(8,128)(2,1)}, u32[]{:S(2)}) copy-start(bf16[512,128]{1,0:T(8,128)(2,1)} %get-tuple-element.10.out_f) | copy-start | bytes 393220

commit v3 on v2

--- a/solution.py
+++ b/solution.py
@@ -1,4 +1,5 @@
 import functools
+import math
 
 import jax
 import jax.numpy as jnp
@@ -13,58 +14,11 @@
 MIB = 1024 * 1024
 
 
-def project_kernel(steps, lengths, act, og, w_in, w_out, in_f, out_f, in_acc, out_acc):
-    step = pl.program_id(0)
-    in_part = jnp.dot(act[...], w_in[...], preferred_element_type=jnp.float32)
-    out_part = jnp.dot(og[...], w_out[...], preferred_element_type=jnp.float32)
-
-    @pl.when(step == 0)
-    def _():
-        in_acc[...] = in_part
-        out_acc[...] = out_part
-
-    @pl.when(step > 0)
-    def _():
-        in_acc[...] += in_part
-        out_acc[...] += out_part
-
-    @pl.when(step == steps - 1)
-    def _():
-        in_f[...] = in_acc[...].astype(in_f.dtype)
-        place = lax.broadcasted_iota(jnp.int32, (L, out_f.shape[1]), 0)
-        for e in range(out_f.shape[0] // L):
-            rows = pl.ds(e * L, L)
-            kept = jnp.where(place < lengths[e], out_acc[rows, :], 0.0)
-            out_f[rows, :] = kept.astype(out_f.dtype)
-
-
-def project(activations, out_grads, lengths, proj_in, proj_out):
-    steps = 4
-    tokens, width = activations.shape[0], proj_in.shape[1]
-    deep_in, deep_out = activations.shape[1] // steps, out_grads.shape[1] // steps
-    factors = jax.ShapeDtypeStruct((tokens, width), jnp.bfloat16)
-    whole = pl.BlockSpec((tokens, width), lambda s: (0, 0))
-    return pl.pallas_call(
-        functools.partial(project_kernel, steps),
-        grid=(steps,),
-        in_specs=[
-            pl.BlockSpec(memory_space=pltpu.SMEM),
-            pl.BlockSpec((tokens, deep_in), lambda s: (0, s)),
-            pl.BlockSpec((tokens, deep_out), lambda s: (0, s)),
-            pl.BlockSpec((deep_in, width), lambda s: (s, 0)),
-            pl.BlockSpec((deep_out, width), lambda s: (s, 0)),
-        ],
-        out_specs=[whole, whole],
-        out_shape=[factors, factors],
-        scratch_shapes=[pltpu.VMEM((tokens, width), jnp.float32)] * 2,
-        compiler_params=pltpu.CompilerParams(vmem_limit_bytes=60 * MIB),
-    )(lengths, activations, out_grads, proj_in, proj_out)
-
-
 def exchange_kernel(
-    n, in_f, out_f, row_ref, col_ref,
-    in_peer, out_peer, wide, blocks,
-    peer_s, peer_r, c1_s, c1_r, r1_s, r1_r, line_s, line_r, c2_s, c2_r, fw_s, fw_r, own_s,
+    n, lengths, act, og, w_in, w_out, row_ref, col_ref,
+    act_v, og_v, w_in_v, w_out_v, in_acc, out_acc,
+    in_f, out_f, in_peer, out_peer, wide, blocks,
+    load_s, peer_s, peer_r, c1_s, c1_r, r1_s, r1_r, line_s, line_r, c2_s, c2_r, fw_s, fw_r, own_s,
 ):
     r, c = lax.axis_index("row"), lax.axis_index("col")
     k, m = r // CORES, r % CORES
@@ -74,6 +28,29 @@
     pair_ex = CORES * local_ex
     per_block = blocks.shape[2] // width
 
+    def loads(x, w, x_v, w_v, first):
+        depth = x_v.shape[2]
+        return [
+            (
+                pltpu.make_async_copy(x.at[:, pl.ds(q * depth, depth)], x_v.at[q], load_s.at[first + q, 0]),
+                pltpu.make_async_copy(w.at[pl.ds(q * depth, depth)], w_v.at[q], load_s.at[first + q, 1]),
+            )
+            for q in range(x_v.shape[0])
+        ]
+
+    act_loads = loads(act, w_in, act_v, w_in_v, 0)
+    og_loads = loads(og, w_out, og_v, w_out_v, len(act_loads))
+    for pair in act_loads + og_loads:
+        for copy in pair:
+            copy.start()
+
+    def project(pairs, x_v, w_v, acc):
+        for q, pair in enumerate(pairs):
+            for copy in pair:
+                copy.wait()
+            part = jnp.dot(x_v[q], w_v[q], preferred_element_type=jnp.float32)
+            acc[...] = part if q == 0 else acc[...] + part
+
     def turn(start, d):
         return lax.rem(start + d + n, n)
 
@@ -89,12 +66,18 @@
     for d in range(1, n):
         pl.semaphore_signal(barrier, inc=1, device_id=(turn(k, d) * CORES + m, c), device_id_type=MESH)
         pl.semaphore_signal(barrier, inc=1, device_id=(r, turn(c, d)), device_id_type=MESH)
+
+    project(act_loads, act_v, w_in_v, in_acc)
+    in_f[...] = in_acc[...].astype(in_f.dtype)
     pl.semaphore_wait(barrier, 2 * n - 1)
-
-    swaps = [
-        send(in_f, in_peer, peer_s.at[0], peer_r.at[0], peer),
-        send(out_f, out_peer, peer_s.at[1], peer_r.at[1], peer),
-    ]
+    swaps = [send(in_f, in_peer, peer_s.at[0], peer_r.at[0], peer)]
+
+    project(og_loads, og_v, w_out_v, out_acc)
+    place = lax.broadcasted_iota(jnp.int32, (L, width), 0)
+    for e in range(local_ex):
+        rows = pl.ds(e * L, L)
+        out_f[rows, :] = jnp.where(place < lengths[e], out_acc[rows, :], 0.0).astype(out_f.dtype)
+    swaps.append(send(out_f, out_peer, peer_s.at[1], peer_r.at[1], peer))
 
     def outer(ins, outs, core):
         for e in range(local_ex):
@@ -102,8 +85,8 @@
             grad = lax.dot_general(
                 outs[rows, :], ins[rows, :], (((0,), (0,)), ((), ())), preferred_element_type=jnp.float32
             )
-            place = pl.multiple_of((core * local_ex + e) * width, width)
-            wide[pl.ds(place, width), :] = grad * (1.0 / jnp.sqrt(jnp.float32(L)))
+            start = pl.multiple_of((core * local_ex + e) * width, width)
+            wide[pl.ds(start, width), :] = grad * (1.0 / jnp.sqrt(jnp.float32(L)))
 
     outer(in_f, out_f, m)
     for copy in swaps:
@@ -209,27 +192,36 @@
         copy.wait()
 
 
-def exchange(in_f, out_f, n_row, n_col):
+def exchange(activations, out_grads, lengths, proj_in, proj_out, n_row, n_col):
     n = n_col
     assert n_row == CORES * n
-    tokens, width = in_f.shape
+    tokens, width = activations.shape[0], proj_in.shape[1]
     pair_ex = CORES * (tokens // L)
     block = width * width // n_row
+    depth = math.gcd(proj_in.shape[0], proj_out.shape[0])
+    ins, outs = proj_in.shape[0] // depth, proj_out.shape[0] // depth
     dma = pltpu.SemaphoreType.DMA
     anywhere = pl.BlockSpec(memory_space=pl.ANY)
     return pl.pallas_call(
         functools.partial(exchange_kernel, n),
-        in_specs=[pl.BlockSpec(memory_space=pltpu.VMEM)] * 2,
+        in_specs=[pl.BlockSpec(memory_space=pltpu.SMEM)] + [anywhere] * 4,
         out_specs=[anywhere, anywhere],
         out_shape=[
             jax.ShapeDtypeStruct((n, n, pair_ex, block), jnp.bfloat16),
             jax.ShapeDtypeStruct((CORES, n, n, pair_ex, block), jnp.bfloat16),
         ],
         scratch_shapes=[
-            pltpu.VMEM((tokens, width), jnp.bfloat16),
-            pltpu.VMEM((tokens, width), jnp.bfloat16),
+            pltpu.VMEM((ins, tokens, depth), jnp.bfloat16),
+            pltpu.VMEM((outs, tokens, depth), jnp.bfloat16),
+            pltpu.VMEM((ins, depth, width), jnp.bfloat16),
+            pltpu.VMEM((outs, depth, width), jnp.bfloat16),
+        ]
+        + [pltpu.VMEM((tokens, width), jnp.float32)] * 2
+        + [pltpu.VMEM((tokens, width), jnp.bfloat16)] * 4
+        + [
             pltpu.VMEM((pair_ex * width, width), jnp.float32),
             pltpu.VMEM((n, pair_ex, block), jnp.bfloat16),
+            dma((ins + outs, 2)),
             dma((2,)), dma((2,)),
         ]
         + [dma((n,))] * 4
@@ -237,9 +229,9 @@
         + [dma((n,))] * 4
         + [dma((2,))],
         compiler_params=pltpu.CompilerParams(
-            collective_id=0, has_side_effects=True, vmem_limit_bytes=32 * MIB
+            collective_id=0, has_side_effects=True, vmem_limit_bytes=58 * MIB
         ),
-    )(in_f, out_f)
+    )(lengths, activations, out_grads, proj_in, proj_out)
 
 
 def fisher_kernel(scale, slots, parts, left, right, out, held, sems):
@@ -298,7 +290,7 @@
             pltpu.VMEM((slots, tile, block), jnp.float32),
             pltpu.SemaphoreType.DMA((slots, parts)),
         ],
-        compiler_params=pltpu.CompilerParams(vmem_limit_bytes=24 * MIB),
+        compiler_params=pltpu.CompilerParams(vmem_limit_bytes=60 * MIB),
     )(row_all, col_all)
 
 
@@ -306,10 +298,11 @@
     tokens = activations.shape[0] * L
     n_row = lax.axis_size("row")
     n_col = lax.axis_size("col")
-    in_f, out_f = project(
-        activations.reshape(tokens, -1), out_grads.reshape(tokens, -1), lengths, proj_in, proj_out
+    row_all, col_all = exchange(
+        activations.reshape(tokens, -1),
+        out_grads.reshape(tokens, -1),
+        lengths, proj_in, proj_out, n_row, n_col,
     )
-    row_all, col_all = exchange(in_f, out_f, n_row, n_col)
     block = row_all.shape[-1]
     return fisher(row_all.reshape(-1, block), col_all.reshape(CORES, -1, block))
 

time: 54.6 us -> 56.9 us (1.042)
  Pallas kernels: 52.7 us -> 56.4 us
  local copies, waits for them, and re-layouts: 1.81 us -> 0 us
    pallas_call x1 -> x0, Pallas kernels: 8.75 us -> none  [project(): pl.pallas_call(functools.partial(project_kernel, steps), grid=(steps,), i...]
    pallas_call x1, Pallas kernels: 32.5 us -> 40.7 us  [exchange(): pl.pallas_call(functools.partial(exchange_kernel, n), in_specs=[pl.BlockS...]
    pallas_call x1, Pallas kernels: 11.5 us -> 15.7 us  [fisher(): pl.pallas_call(functools.partial(fisher_kernel, 1.0 / total ** 0.5, slots...]
    unnamed x4 -> x0, local copies, waits for them, and re-layouts: 1.81 us -> none
where the time goes in v3:
time: 56.9 us; the launch traced here: 56.5 us
  Pallas kernels  56.4 us (99%)
    pallas_call x1, Pallas kernels, exchange(): pl.pallas_call(functools.partial(exchange_kernel, n), in_specs=[pl.BlockS...  40.7 us
    pallas_call x1, Pallas kernels, fisher(): pl.pallas_call(functools.partial(fisher_kernel, 1.0 / total ** 0.5, slots...  15.7 us

profile of v3, /device:TPU:0, one launch (start us, length us, event | category | flops | bytes accessed | tf_op | source)
XLA Modules:
  0.0 56.5 jit_solution(17094619130036303913)
XLA Ops:
  0.0 40.7 %shard_map.55 = (bf16[4,4,16,2048]{3,2,1,0:T(8,128)(2,1)}, bf16[2,4,4,16,2048]{4,3,2,1,0:T(8,128)(2,1)}) custom-call(s32[8]{0:T(128)} %lengths.1, bf16[512,5120]{1,0:T(8,128)(2,1)} %bitcast.5, bf16[512,8192]{1,0:T(8,128)(2,1)} %bitcast.4, bf16[5120,128]{1,0:T(8,128)(2,1)} %w_in.1, bf16[8192,128]{1,0:T(8,128)(2,1)} %w_out.1), custom_call_target="tpu_custom_call" | custom-call | tf_op jit(solution)/shard_map/pallas_call | solution.py:205
  40.7 15.7 %shard_map.56 = f32[2048,4096]{1,0:T(8,128)} custom-call(bf16[256,2048]{1,0:T(8,128)(2,1)} %bitcast.7, bf16[2,256,2048]{2,1,0:T(8,128)(2,1)} %bitcast.6), custom_call_target="tpu_custom_call" | custom-call | tf_op jit(solution)/shard_map/pallas_call | solution.py:280

commit v4 on v3

--- a/solution.py
+++ b/solution.py
@@ -173,11 +173,13 @@
         send(mine, mine, c2_s.at[d], c2_r.at[d], (turn(k, d) * CORES + m, c)) for d in range(1, n)
     ]
     passed = [send(mine, mine, fw_s.at[0], fw_r.at[0], peer)]
+    for t in range(1, n - 1):
+        relay(t)
     for d in range(1, n):
-        relay(d)
         across[d - 1].wait_recv()
         piece = col_ref.at[m, :, turn(k, -d)]
         passed.append(send(piece, piece, fw_s.at[d], fw_r.at[d], peer))
+    relay(n - 1)
     for copy in across:
         copy.wait_send()
     for t in range(n - 1):
@@ -201,11 +203,10 @@
     depth = math.gcd(proj_in.shape[0], proj_out.shape[0])
     ins, outs = proj_in.shape[0] // depth, proj_out.shape[0] // depth
     dma = pltpu.SemaphoreType.DMA
-    anywhere = pl.BlockSpec(memory_space=pl.ANY)
     return pl.pallas_call(
         functools.partial(exchange_kernel, n),
-        in_specs=[pl.BlockSpec(memory_space=pltpu.SMEM)] + [anywhere] * 4,
-        out_specs=[anywhere, anywhere],
+        in_specs=[pl.BlockSpec(memory_space=pltpu.SMEM)] + [pl.BlockSpec(memory_space=pl.ANY)] * 4,
+        out_specs=[pl.BlockSpec(memory_space=pl.ANY)] * 2,
         out_shape=[
             jax.ShapeDtypeStruct((n, n, pair_ex, block), jnp.bfloat16),
             jax.ShapeDtypeStruct((CORES, n, n, pair_ex, block), jnp.bfloat16),
@@ -234,7 +235,7 @@
     )(lengths, activations, out_grads, proj_in, proj_out)
 
 
-def fisher_kernel(scale, slots, parts, left, right, out, held, sems):
+def fisher_kernel(scale, slots, parts, left_h, right_h, out, left, right, held, sems, load_s):
     h, i = pl.program_id(0), pl.program_id(1)
     tiles = pl.num_programs(1)
     steps = pl.num_programs(0) * tiles
@@ -254,6 +255,22 @@
             for p in range(parts)
         ]
 
+    loads = [pltpu.make_async_copy(left_h, left, load_s.at[0])] + [
+        pltpu.make_async_copy(right_h.at[s], right.at[s], load_s.at[1 + s]) for s in range(CORES)
+    ]
+
+    @pl.when(step == 0)
+    def _():
+        for copy in loads:
+            copy.start()
+        loads[0].wait()
+
+    for s in range(CORES):
+
+        @pl.when(step == s * tiles)
+        def _(s=s):
+            loads[1 + s].wait()
+
     @pl.when(step >= slots)
     def _():
         for copy in writes(step - slots):
@@ -261,7 +278,7 @@
 
     slot = lax.rem(step, slots)
     held[slot] = scale * lax.dot_general(
-        left[...], right[0], (((0,), (0,)), ((), ())), preferred_element_type=jnp.float32
+        left[:, pl.ds(pl.multiple_of(i * tile, tile), tile)], right[h], (((0,), (0,)), ((), ())), preferred_element_type=jnp.float32
     )
     for copy in writes(step):
         copy.start()
@@ -281,14 +298,17 @@
         functools.partial(fisher_kernel, 1.0 / total**0.5, slots, parts),
         grid=(halves, rows // tile),
         in_specs=[
-            pl.BlockSpec((total, tile), lambda h, i: (0, i)),
-            pl.BlockSpec((1, total, block), lambda h, i: (h, 0, 0)),
+            pl.BlockSpec(memory_space=pl.ANY),
+            pl.BlockSpec(memory_space=pl.ANY),
         ],
         out_specs=pl.BlockSpec(memory_space=pl.ANY),
         out_shape=jax.ShapeDtypeStruct((rows, halves * block), jnp.float32),
         scratch_shapes=[
+            pltpu.VMEM(row_all.shape, row_all.dtype),
+            pltpu.VMEM(col_all.shape, col_all.dtype),
             pltpu.VMEM((slots, tile, block), jnp.float32),
             pltpu.SemaphoreType.DMA((slots, parts)),
+            pltpu.SemaphoreType.DMA((1 + halves,)),
         ],
         compiler_params=pltpu.CompilerParams(vmem_limit_bytes=60 * MIB),
     )(row_all, col_all)

time: 56.9 us -> 52.4 us (0.921)
  Pallas kernels: 56.4 us -> 52.2 us
    pallas_call x1, Pallas kernels: 15.7 us -> 13 us  [fisher(): pl.pallas_call(functools.partial(fisher_kernel, 1.0 / total ** 0.5, slots...]
    pallas_call x1, Pallas kernels: 40.7 us -> 39.2 us  [exchange(): pl.pallas_call(functools.partial(exchange_kernel, n), in_specs=[pl.BlockS...]
where the time goes in v4:
time: 52.4 us; the launch traced here: 52.2 us
  Pallas kernels  52.2 us (100%)
    pallas_call x1, Pallas kernels, exchange(): pl.pallas_call(functools.partial(exchange_kernel, n), in_specs=[pl.BlockS...  39.2 us
    pallas_call x1, Pallas kernels, fisher(): pl.pallas_call(functools.partial(fisher_kernel, 1.0 / total ** 0.5, slots...  13 us

profile of v4, /device:TPU:0, one launch (start us, length us, event | category | flops | bytes accessed | tf_op | source)
XLA Modules:
  0.0 52.2 jit_solution(18256219043183932013)
XLA Ops:
  0.0 39.2 %shard_map.55 = (bf16[4,4,16,2048]{3,2,1,0:T(8,128)(2,1)}, bf16[2,4,4,16,2048]{4,3,2,1,0:T(8,128)(2,1)}) custom-call(s32[8]{0:T(128)} %lengths.1, bf16[512,5120]{1,0:T(8,128)(2,1)} %bitcast.5, bf16[512,8192]{1,0:T(8,128)(2,1)} %bitcast.4, bf16[5120,128]{1,0:T(8,128)(2,1)} %w_in.1, bf16[8192,128]{1,0:T(8,128)(2,1)} %w_out.1), custom_call_target="tpu_custom_call" | custom-call | tf_op jit(solution)/shard_map/pallas_call | solution.py:206
  39.2 13.0 %shard_map.56 = f32[2048,4096]{1,0:T(8,128)} custom-call(bf16[256,2048]{1,0:T(8,128)(2,1)} %bitcast.7, bf16[2,256,2048]{2,1,0:T(8,128)(2,1)} %bitcast.6), custom_call_target="tpu_custom_call" | custom-call | tf_op jit(solution)/shard_map/pallas_call | solution.py:297

commit v5 on v4

--- a/solution.py
+++ b/solution.py
@@ -93,7 +93,7 @@
         copy.wait()
     outer(in_peer, out_peer, 1 - m)
 
-    for q in range(n):
+    def form(q):
         for i in range(per_block):
             first = (q * CORES + m) * per_block + i
             blocks[q, :, i * width : (i + 1) * width] = wide[
@@ -103,7 +103,10 @@
     to_col, to_row = [], []
     for d in range(1, n):
         q = turn(c, d)
+        form(q)
         to_col.append(send(blocks.at[q], col_ref.at[m, c, k], c1_s.at[d], c1_r.at[d], (r, q)))
+    form(c)
+    for d in range(1, n):
         q = turn(k, d)
         to_row.append(send(blocks.at[q], row_ref.at[c, k], r1_s.at[d], r1_r.at[d], (q * CORES + m, c)))
     own = [
@@ -112,6 +115,14 @@
     ]
     for copy in own:
         copy.start()
+
+    def broadcast(e, src):
+        return [
+            send(src, col_ref.at[m, turn(c, -e), k], c2_s.at[d, e], c2_r.at[d, e], (turn(k, d) * CORES + m, c))
+            for d in range(1, n)
+        ]
+
+    across = [broadcast(0, blocks.at[c])]
 
     half = n // 2
 
@@ -165,22 +176,21 @@
     own[0].wait()
     relay(0)
 
-    for copy in to_col:
-        copy.wait()
+    for e in range(1, n):
+        to_col[e - 1].wait_recv()
+        across.append(broadcast(e, col_ref.at[m, turn(c, -e), k]))
     own[1].wait()
     mine = col_ref.at[m, :, k]
-    across = [
-        send(mine, mine, c2_s.at[d], c2_r.at[d], (turn(k, d) * CORES + m, c)) for d in range(1, n)
-    ]
     passed = [send(mine, mine, fw_s.at[0], fw_r.at[0], peer)]
     for t in range(1, n - 1):
         relay(t)
     for d in range(1, n):
-        across[d - 1].wait_recv()
+        for e in range(n):
+            across[e][d - 1].wait_recv()
         piece = col_ref.at[m, :, turn(k, -d)]
         passed.append(send(piece, piece, fw_s.at[d], fw_r.at[d], peer))
     relay(n - 1)
-    for copy in across:
+    for copy in to_col + sum(across, []):
         copy.wait_send()
     for t in range(n - 1):
         for way in (1, -1):
@@ -227,7 +237,8 @@
         ]
         + [dma((n,))] * 4
         + [dma((2, n - 1, 2))] * 2
-        + [dma((n,))] * 4
+        + [dma((n, n))] * 2
+        + [dma((n,))] * 2
         + [dma((2,))],
         compiler_params=pltpu.CompilerParams(
             collective_id=0, has_side_effects=True, vmem_limit_bytes=58 * MIB
@@ -255,21 +266,35 @@
             for p in range(parts)
         ]
 
-    loads = [pltpu.make_async_copy(left_h, left, load_s.at[0])] + [
-        pltpu.make_async_copy(right_h.at[s], right.at[s], load_s.at[1 + s]) for s in range(CORES)
+    early = 2 * tile
+    rest = left.shape[1] - early
+    first = [
+        pltpu.make_async_copy(right_h.at[0], right.at[0], load_s.at[0]),
+        pltpu.make_async_copy(left_h.at[:, pl.ds(0, early)], left.at[:, pl.ds(0, early)], load_s.at[1]),
     ]
+    later = [
+        pltpu.make_async_copy(
+            left_h.at[:, pl.ds(early, rest)], left.at[:, pl.ds(early, rest)], load_s.at[2]
+        ),
+        pltpu.make_async_copy(right_h.at[1], right.at[1], load_s.at[3]),
+    ]
 
     @pl.when(step == 0)
     def _():
-        for copy in loads:
+        for copy in first:
             copy.start()
-        loads[0].wait()
-
-    for s in range(CORES):
-
-        @pl.when(step == s * tiles)
-        def _(s=s):
-            loads[1 + s].wait()
+        for copy in first:
+            copy.wait()
+        for copy in later:
+            copy.start()
+
+    @pl.when(step == 2)
+    def _():
+        later[0].wait()
+
+    @pl.when(step == tiles)
+    def _():
+        later[1].wait()
 
     @pl.when(step >= slots)
     def _():
@@ -308,7 +333,7 @@
             pltpu.VMEM(col_all.shape, col_all.dtype),
             pltpu.VMEM((slots, tile, block), jnp.float32),
             pltpu.SemaphoreType.DMA((slots, parts)),
-            pltpu.SemaphoreType.DMA((1 + halves,)),
+            pltpu.SemaphoreType.DMA((4,)),
         ],
         compiler_params=pltpu.CompilerParams(vmem_limit_bytes=60 * MIB),
     )(row_all, col_all)

time: 52.4 us -> 52.1 us (level)
  no operation moved by 1% of the time
where the time goes in v5:
time: 52.1 us; the launch traced here: 51.9 us
  Pallas kernels  51.9 us (100%)
    pallas_call x1, Pallas kernels, exchange(): pl.pallas_call(functools.partial(exchange_kernel, n), in_specs=[pl.BlockS...  39.2 us
    pallas_call x1, Pallas kernels, fisher(): pl.pallas_call(functools.partial(fisher_kernel, 1.0 / total ** 0.5, slots...  12.7 us

profile of v5, /device:TPU:0, one launch (start us, length us, event | category | flops | bytes accessed | tf_op | source)
XLA Modules:
  0.0 51.9 jit_solution(5281477325534162817)
XLA Ops:
  0.0 39.2 %shard_map.55 = (bf16[4,4,16,2048]{3,2,1,0:T(8,128)(2,1)}, bf16[2,4,4,16,2048]{4,3,2,1,0:T(8,128)(2,1)}) custom-call(s32[8]{0:T(128)} %lengths.1, bf16[512,5120]{1,0:T(8,128)(2,1)} %bitcast.5, bf16[512,8192]{1,0:T(8,128)(2,1)} %bitcast.4, bf16[5120,128]{1,0:T(8,128)(2,1)} %w_in.1, bf16[8192,128]{1,0:T(8,128)(2,1)} %w_out.1), custom_call_target="tpu_custom_call" | custom-call | tf_op jit(solution)/shard_map/pallas_call | solution.py:216
  39.2 12.7 %shard_map.56 = f32[2048,4096]{1,0:T(8,128)} custom-call(bf16[256,2048]{1,0:T(8,128)(2,1)} %bitcast.7, bf16[2,256,2048]{2,1,0:T(8,128)(2,1)} %bitcast.6), custom_call_target="tpu_custom_call" | custom-call | tf_op jit(solution)/shard_map/pallas_call | solution.py:322

commit v6 on v5

--- a/solution.py
+++ b/solution.py
@@ -17,14 +17,15 @@
 def exchange_kernel(
     n, lengths, act, og, w_in, w_out, row_ref, col_ref,
     act_v, og_v, w_in_v, w_out_v, in_acc, out_acc,
-    in_f, out_f, in_peer, out_peer, wide, blocks,
+    ins, outs, flipped, spread, blocks,
     load_s, peer_s, peer_r, c1_s, c1_r, r1_s, r1_r, line_s, line_r, c2_s, c2_r, fw_s, fw_r, own_s,
 ):
     r, c = lax.axis_index("row"), lax.axis_index("col")
     k, m = r // CORES, r % CORES
     peer = (k * CORES + 1 - m, c)
-    width = in_f.shape[1]
-    local_ex = in_f.shape[0] // L
+    width = ins.shape[1]
+    tokens = act.shape[0]
+    local_ex = tokens // L
     pair_ex = CORES * local_ex
     per_block = blocks.shape[2] // width
 
@@ -68,37 +69,43 @@
         pl.semaphore_signal(barrier, inc=1, device_id=(r, turn(c, d)), device_id_type=MESH)
 
     project(act_loads, act_v, w_in_v, in_acc)
-    in_f[...] = in_acc[...].astype(in_f.dtype)
+    own_rows = pl.ds(pl.multiple_of(m * tokens, tokens), tokens)
+    ins[own_rows, :] = in_acc[...].astype(ins.dtype)
     pl.semaphore_wait(barrier, 2 * n - 1)
-    swaps = [send(in_f, in_peer, peer_s.at[0], peer_r.at[0], peer)]
+    swaps = [send(ins.at[own_rows], ins.at[own_rows], peer_s.at[0], peer_r.at[0], peer)]
 
     project(og_loads, og_v, w_out_v, out_acc)
     place = lax.broadcasted_iota(jnp.int32, (L, width), 0)
     for e in range(local_ex):
         rows = pl.ds(e * L, L)
-        out_f[rows, :] = jnp.where(place < lengths[e], out_acc[rows, :], 0.0).astype(out_f.dtype)
-    swaps.append(send(out_f, out_peer, peer_s.at[1], peer_r.at[1], peer))
-
-    def outer(ins, outs, core):
-        for e in range(local_ex):
-            rows = pl.ds(e * L, L)
-            grad = lax.dot_general(
-                outs[rows, :], ins[rows, :], (((0,), (0,)), ((), ())), preferred_element_type=jnp.float32
-            )
-            start = pl.multiple_of((core * local_ex + e) * width, width)
-            wide[pl.ds(start, width), :] = grad * (1.0 / jnp.sqrt(jnp.float32(L)))
-
-    outer(in_f, out_f, m)
+        out_acc[rows, :] = jnp.where(place < lengths[e], out_acc[rows, :], 0.0)
+    outs[own_rows, :] = out_acc[...].astype(outs.dtype)
+    swaps.append(send(outs.at[own_rows], outs.at[own_rows], peer_s.at[1], peer_r.at[1], peer))
+
+    def flip(core):
+        span = pl.ds(pl.multiple_of(core * tokens, tokens), tokens)
+        flipped[:, span] = outs[span, :].astype(jnp.float32).T
+
+    flip(m)
     for copy in swaps:
         copy.wait()
-    outer(in_peer, out_peer, 1 - m)
+    flip(1 - m)
+
+    whose = lax.broadcasted_iota(jnp.int32, (pair_ex, CORES * tokens), 1) // L
+    mine_only = whose == lax.broadcasted_iota(jnp.int32, (pair_ex, CORES * tokens), 0)
 
     def form(q):
+        first = pl.multiple_of((q * CORES + m) * per_block, per_block)
+        group = flipped[pl.ds(first, per_block), :]
         for i in range(per_block):
-            first = (q * CORES + m) * per_block + i
-            blocks[q, :, i * width : (i + 1) * width] = wide[
-                pl.ds(first, pair_ex, stride=width), :
-            ].astype(blocks.dtype)
+            line = jnp.broadcast_to(group[i : i + 1, :], mine_only.shape)
+            spread[pl.ds(i * pair_ex, pair_ex), :] = jnp.where(mine_only, line, 0.0).astype(spread.dtype)
+        grad = jnp.dot(spread[...], ins[...], preferred_element_type=jnp.float32)
+        grad = grad * (1.0 / jnp.sqrt(jnp.float32(L)))
+        for i in range(per_block):
+            blocks[q, :, i * width : (i + 1) * width] = grad[i * pair_ex : (i + 1) * pair_ex, :].astype(
+                blocks.dtype
+            )
 
     to_col, to_row = [], []
     for d in range(1, n):
@@ -228,9 +235,10 @@
             pltpu.VMEM((outs, depth, width), jnp.bfloat16),
         ]
         + [pltpu.VMEM((tokens, width), jnp.float32)] * 2
-        + [pltpu.VMEM((tokens, width), jnp.bfloat16)] * 4
+        + [pltpu.VMEM((CORES * tokens, width), jnp.bfloat16)] * 2
         + [
-            pltpu.VMEM((pair_ex * width, width), jnp.float32),
+            pltpu.VMEM((width, CORES * tokens), jnp.float32),
+            pltpu.VMEM((width // n_row * pair_ex, CORES * tokens), jnp.bfloat16),
             pltpu.VMEM((n, pair_ex, block), jnp.bfloat16),
             dma((ins + outs, 2)),
             dma((2,)), dma((2,)),

time: 52.1 us -> 52.8 us (1.013)
  Pallas kernels: 51.9 us -> 52.7 us
    pallas_call x1, Pallas kernels: 39.2 us -> 40 us  [exchange(): pl.pallas_call(functools.partial(exchange_kernel, n), in_specs=[pl.BlockS...]
where the time goes in v6:
time: 52.8 us; the launch traced here: 52.7 us
  Pallas kernels  52.7 us (100%)
    pallas_call x1, Pallas kernels, exchange(): pl.pallas_call(functools.partial(exchange_kernel, n), in_specs=[pl.BlockS...  40 us
    pallas_call x1, Pallas kernels, fisher(): pl.pallas_call(functools.partial(fisher_kernel, 1.0 / total ** 0.5, slots...  12.7 us

profile of v6, /device:TPU:0, one launch (start us, length us, event | category | flops | bytes accessed | tf_op | source)
XLA Modules:
  0.0 52.7 jit_solution(4110062940198979639)
XLA Ops:
  0.0 40.0 %shard_map.55 = (bf16[4,4,16,2048]{3,2,1,0:T(8,128)(2,1)}, bf16[2,4,4,16,2048]{4,3,2,1,0:T(8,128)(2,1)}) custom-call(s32[8]{0:T(128)} %lengths.1, bf16[512,5120]{1,0:T(8,128)(2,1)} %bitcast.5, bf16[512,8192]{1,0:T(8,128)(2,1)} %bitcast.4, bf16[5120,128]{1,0:T(8,128)(2,1)} %w_in.1, bf16[8192,128]{1,0:T(8,128)(2,1)} %w_out.1), custom_call_target="tpu_custom_call" | custom-call | tf_op jit(solution)/shard_map/pallas_call | solution.py:223
  40.0 12.7 %shard_map.56 = f32[2048,4096]{1,0:T(8,128)} custom-call(bf16[256,2048]{1,0:T(8,128)(2,1)} %bitcast.7, bf16[2,256,2048]{2,1,0:T(8,128)(2,1)} %bitcast.6), custom_call_target="tpu_custom_call" | custom-call | tf_op jit(solution)/shard_map/pallas_call | solution.py:330
